TPU v7x, 32 devices: a whole 2x2x4 slice. The times are simulated.
32 devices in a mesh: dom: 8 (over z, x), sub: 4 (over y, core).
Axes of the slice: x: 2, y: 2, z: 4, core: 2. Of those that a mesh axis runs over, the one named last changes fastest.
Arguments:
- adjoint_field: float32 [4096, 5, 512], P(('dom', 'sub')), may hold values from -6 to 6
- metric: float32 [4096, 3, 512], P(('dom', 'sub')), may hold values from 0.5 to 4
- velocity: float32 [4096, 3, 512], P(('dom', 'sub')), may hold values from -2 to 2
- mortar_route: int32 [4096, 1], P(('dom', 'sub')), may hold values from 0 to 7, as said below
- mortar_element: int32 [4096, 1], P(('dom', 'sub')), may hold values from 0 to 127
- face_code: int32 [4096, 1], P(('dom', 'sub')), may hold values from 0 to 7
- hanging: int32 [4096, 1], P(('dom', 'sub')), may hold values 0 or 1
Outputs:
- result: float32 [4096, 5, 512], P(('dom', 'sub'))
Inputs may be any that keep to these rules, and one draw needn't show every extreme that they name: `mortar_route`: each element's value is its own device's dom index d or one of d - 2, d - 1, d + 1, d + 2 taken modulo 8. In each aligned block of 128 rows (the elements of one device) no value is named by more than 96 rows, and some value by exactly 96.
All inputs are finite; a program needn't handle non-finite values. No bound on the sum of `hanging` on one device may be relied on, other than what follows from the above.
Results may differ from a plain program's by a relative error of at most 0.00088.
Values may be sent and summed in bfloat16 or wider, within the bound.
No kernel may reach another device: no remote copies, remote signals or barrier semaphores. Data moves between devices by JAX's collectives and lax.ppermute only.
A program may use at most 64 MiB of HBM per device.

v0:
```python
import jax
import jax.numpy as jnp
import numpy as np
from jax import lax
from jax.sharding import PartitionSpec as P

gll_nodes = np.array(
    [
        -1.0,
        -0.8717401485096066,
        -0.5917001814331423,
        -0.2092992179024789,
        0.2092992179024789,
        0.5917001814331423,
        0.8717401485096066,
        1.0,
    ]
)
viscosity = 0.005


def passed_along(block, axis, distance):
    devices = range(lax.axis_size(axis))
    route = [((i - distance) % len(devices), i) for i in devices]
    return lax.ppermute(block, axis, route)


def extended(block, sides, width):
    for axis, dim in sides:
        count = lax.axis_size(axis)
        forward = [(i, i + 1) for i in range(count - 1)]
        backward = [(target, source) for source, target in forward]
        low = lax.ppermute(
            lax.slice_in_dim(block, block.shape[dim] - width, None, axis=dim), axis, forward
        )
        high = lax.ppermute(lax.slice_in_dim(block, 0, width, axis=dim), axis, backward)
        block = jnp.concatenate([low, block, high], axis=dim)
    return block


def legendre_seven(points):
    prev = np.ones(points.shape)
    curr = np.array(points)
    for order in range(1, 7):
        nxt = ((2 * order + 1) * points * curr - order * prev) / (order + 1)
        prev, curr = (curr, nxt)
    return curr


def diff_matrix():
    values = legendre_seven(gll_nodes)
    result_mat = np.zeros((8, 8))
    for row in range(8):
        for col in range(8):
            if row != col:
                result_mat[row, col] = values[row] / (
                    values[col] * (gll_nodes[row] - gll_nodes[col])
                )
    result_mat[0, 0] = -14.0
    result_mat[7, 7] = 14.0
    return result_mat


def lagrange_at(points):
    basis = np.ones((8, 8))
    for row in range(8):
        for col in range(8):
            for other in range(8):
                if other != col:
                    basis[row, col] *= (points[row] - gll_nodes[other]) / (
                        gll_nodes[col] - gll_nodes[other]
                    )
    return basis


def face_tables():
    halves = [lagrange_at((gll_nodes - 1.0) / 2.0), lagrange_at((gll_nodes + 1.0) / 2.0)]
    perm_mat = np.zeros((64, 64))
    for col in range(64):
        perm_mat[col % 8 * 8 + col // 8, col] = 1.0
    tables = []
    for code in range(8):
        mat = np.kron(halves[code % 2], halves[code // 2 % 2])
        if code >= 4:
            mat = mat @ perm_mat
        tables.append(mat)
    return np.stack(tables).astype(np.float32)


def kron_tables():
    dmat = diff_matrix()
    eye_eight = np.eye(8)
    first = np.kron(np.kron(eye_eight, dmat), eye_eight)
    second = np.kron(np.kron(eye_eight, eye_eight), dmat)
    return (dmat.astype(np.float32), first.astype(np.float32), second.astype(np.float32))


def fold_faces(fine, codes):
    tables = jnp.asarray(face_tables())
    total = jnp.zeros(fine.shape, jnp.float32)
    for code in range(8):
        mapped = jnp.einsum("efa,ab->efb", fine, tables[code], precision=lax.Precision.HIGHEST)
        total = total + jnp.where((codes == code)[:, :, None], mapped, 0.0)
    return total


def derive(field, dim, mats):
    dmat, first, second = mats
    count = field.shape[0]
    if dim == 0:
        cube = field.reshape(count, 5, 8, 64)
        return jnp.einsum("ai,efip->efap", dmat, cube, precision=lax.Precision.HIGHEST).reshape(
            count, 5, 512
        )
    kron_mat = first if dim == 1 else second
    return jnp.einsum("efp,qp->efq", field, kron_mat, precision=lax.Precision.HIGHEST)


def derive_back(field, dim, mats):
    dmat, first, second = mats
    count = field.shape[0]
    if dim == 0:
        cube = field.reshape(count, 5, 8, 64)
        return jnp.einsum("ai,efap->efip", dmat, cube, precision=lax.Precision.HIGHEST).reshape(
            count, 5, 512
        )
    kron_mat = first if dim == 1 else second
    return jnp.einsum("efq,qp->efp", field, kron_mat, precision=lax.Precision.HIGHEST)


def apply_adjoint(summed, metric, velocity):
    mats = tuple((jnp.asarray(m) for m in kron_tables()))
    total = jnp.zeros(summed.shape, jnp.float32)
    for dim in range(3):
        inner = (
            viscosity * metric[:, dim : dim + 1] * derive(summed, dim, mats)
            + velocity[:, dim : dim + 1] * summed
        )
        total = total + derive_back(inner, dim, mats)
    return total


def shards(adjoint_field, metric, velocity, mortar_route, mortar_element, face_code, hanging):
    elems = adjoint_field.shape[0]
    field_cube = adjoint_field.reshape(elems, 5, 8, 8, 8)
    fine = field_cube[:, :, :, 7, :].reshape(elems, 5, 64)
    hang_f = hanging.astype(jnp.float32)
    folded = (
        (fold_faces(fine, face_code) * hang_f[:, :, None]).astype(jnp.bfloat16).reshape(elems, 320)
    )
    local_ids = jnp.arange(elems, dtype=jnp.int32)
    peers = lax.axis_size("dom")
    cap = max(2, 3 * elems // 4)
    offset_slot = (mortar_route[:, 0] - lax.axis_index("dom") + 2 + peers) % peers
    onehot = (offset_slot[:, None] == jnp.arange(5, dtype=jnp.int32)[None, :]).astype(jnp.int32)
    rank = jnp.sum(jnp.cumsum(onehot, axis=0) * onehot, axis=1) - 1
    slot = offset_slot * cap + rank
    select_int = (slot[None, :] == jnp.arange(5 * cap, dtype=jnp.int32)[:, None]).astype(jnp.int32)
    send_faces = (
        jnp.dot(select_int.astype(jnp.bfloat16), folded, preferred_element_type=jnp.float32)
        .astype(jnp.bfloat16)
        .reshape(5, cap, 320)
    )
    send_dest = (jnp.sum(select_int * (mortar_element[:, 0] + 1)[None, :], axis=1) - 1).reshape(
        5, cap
    )

    def absorb(total, faces, dest):
        hit = (dest[None, :] == local_ids[:, None]).astype(jnp.bfloat16)
        return total + jnp.dot(hit, faces, preferred_element_type=jnp.float32)

    mortar = absorb(jnp.zeros((elems, 320), jnp.float32), send_faces[2], send_dest[2])
    for position, offset in ((0, -2), (1, -1), (3, 1), (4, 2)):
        got_faces, got_dest = passed_along(
            (send_faces[position], send_dest[position]), "dom", offset
        )
        mortar = absorb(mortar, got_faces, got_dest)
    keep = (1.0 - hang_f)[:, :, None, None]
    field_cube = field_cube.at[:, :, :, 7, :].set(field_cube[:, :, :, 7, :] * keep)
    field_cube = field_cube.at[:, :, :, 0, :].add(mortar.reshape(elems, 5, 8, 8))
    high_faces = field_cube[:, :, 7]
    low_faces = field_cube[:, :, 0]
    edges = jnp.stack([low_faces[0], high_faces[-1]])
    padded = extended(edges, ((("dom", "sub"), 0),), 1)
    shared = high_faces[:-1] + low_faces[1:]
    new_high = jnp.concatenate([shared, high_faces[-1:] + padded[3:4]], axis=0)
    new_low = jnp.concatenate([low_faces[:1] + padded[0:1], shared], axis=0)
    field_cube = field_cube.at[:, :, 7].set(new_high).at[:, :, 0].set(new_low)
    return apply_adjoint(field_cube.reshape(elems, 5, 512), metric, velocity)


def solution(mesh):
    return jax.shard_map(
        shards,
        mesh=mesh,
        in_specs=(
            P(("dom", "sub"), None, None),
            P(("dom", "sub"), None, None),
            P(("dom", "sub"), None, None),
            P(("dom", "sub"), None),
            P(("dom", "sub"), None),
            P(("dom", "sub"), None),
            P(("dom", "sub"), None),
        ),
        out_specs=P(("dom", "sub"), None, None),
        check_vma=False,
    )
```

profile of v0, /device:TPU:1, one launch (start us, length us, event | category | flops | bytes accessed | tf_op | source)
XLA Modules:
  0.0 75.3 jit_solution(7162786617679893155)
XLA Ops:
  0.0 0.7 add_bitcast_fusion
  0.7 0.7 fusion.49
  1.3 0.1 fusion.39
  1.4 0.2 reduce_window_sum.11
  1.6 0.2 select_reduce_fusion.1
  1.8 0.7 fusion.48
  2.4 0.1 select_reduce_fusion
  2.6 0.6 fusion.56
  3.2 5.1 %collective-permute-start.2 = (s32[96]{0:T(128)}, s32[96]{0:T(128)}, u32[]{:S(2)}, u32[]{:S(2)}) collective-permute-start(s32[96]{0:T(128)} %get-tuple-element.67), channel_id=1, source_target_pairs={{4,0},{8,4},{12,8},{16,12},{20,16},{24,20},{28,24},{0,28},{5,1},{9... | collective-permute-start | bytes 1160 | tf_op jit(solution)/shard_map/ppermute | solution.py:25
  8.3 3.3 %collective-permute-start = (s32[96]{0:T(128)}, s32[96]{0:T(128)}, u32[]{:S(2)}, u32[]{:S(2)}) collective-permute-start(s32[96]{0:T(128)} %get-tuple-element.70), channel_id=1, source_target_pairs={{8,0},{12,4},{16,8},{20,12},{24,16},{28,20},{0,24},{4,28},{9,1},{1... | collective-permute-start | bytes 1160 | tf_op jit(solution)/shard_map/ppermute | solution.py:25
  11.5 0.7 convert_bitcast_fusion
  12.2 0.7 compare_bitcast_fusion
  12.9 1.7 %copy.47 = f32[128,5,512]{0,2,1:T(8,128)S(1)} copy(f32[128,5,512]{2,0,1:T(8,128)} %param.19) | data formatting | bytes 2621440 | tf_op args[0]
  14.7 0.3 convolution_select_fusion.7
  15.0 0.3 fusion.11
  15.3 0.3 fusion.10
  15.6 0.3 fusion.9
  16.0 0.3 fusion.8
  16.3 0.3 fusion.7
  16.6 0.3 fusion.6
  16.9 0.3 fusion.14
  17.2 0.3 convolution_convert_fusion
  17.5 0.1 fusion.55
  17.6 0.1 collective-permute-start.1
  17.7 0.1 fusion.54
  17.8 0.1 copy.80
  18.0 0.1 copy.79
  18.1 0.1 copy.75
  18.3 2.0 %slice_bitcast_fusion = (f32[128,512]{1,0:T(8,128)}, f32[128,1,512]{2,0,1:T(8,128)S(1)}, f32[128,512]{1,0:T(8,128)}) fusion(f32[128,3,512]{2,0,1:T(8,128)} %param.21), kind=kLoop, calls=%fused_computation.32 | loop fusion | bytes 1572864 | tf_op jit(solution)/shard_map/mul | solution.py:137
  20.3 0.2 fusion.37
  20.5 0.1 copy.67
  20.6 0.8 %copy.62 = f32[128,512]{1,0:T(8,128)} copy(f32[128,512]{0,1:T(8,128)S(1)} %multiply_bitcast_fusion.1) | data formatting | bytes 524288 | tf_op jit(solution)/shard_map/mul | solution.py:136
  21.5 0.2 copy.46
  21.6 0.1 copy.78
  21.8 0.2 copy.58
  21.9 2.4 %collective-permute-start.3 = (bf16[96,320]{0,1:T(8,128)(2,1)S(1)}, bf16[96,320]{0,1:T(8,128)(2,1)S(1)}, u32[]{:S(2)}, u32[]{:S(2)}) collective-permute-start(bf16[96,320]{0,1:T(8,128)(2,1)S(1)} %get-tuple-element.63), channel_id=1, source_target_pairs={{4,0},{8,4},{12,8},{16,12},{20,16},{24,20},{28,24},{0,28},{5,1},{9... | collective-permute-start | bytes 184328 | tf_op jit(solution)/shard_map/ppermute | solution.py:25
  24.4 1.4 %collective-permute-start.7 = (bf16[96,320]{0,1:T(8,128)(2,1)S(1)}, bf16[96,320]{0,1:T(8,128)(2,1)S(1)}, u32[]{:S(2)}, u32[]{:S(2)}) collective-permute-start(bf16[96,320]{0,1:T(8,128)(2,1)S(1)} %get-tuple-element.64), channel_id=1, source_target_pairs={{24,0},{28,4},{0,8},{4,12},{8,16},{12,20},{16,24},{20,28},{25,1},{... | collective-permute-start | bytes 184328 | tf_op jit(solution)/shard_map/ppermute | solution.py:25
  25.8 0.9 %convolution_add_fusion.3 = f32[128,320]{0,1:T(8,128)S(1)} fusion(f32[128,320]{0,1:T(8,128)S(1)} %fusion.37, bf16[96,320]{0,1:T(8,128)(2,1)S(1)} %collective-permute-done.1, s32[96]{0:T(128)} %collective-permute-done), kind=kOutput, calls=%fused_computation.30 | convolution fusion | flops 7917568 | bytes 389504 | tf_op jit(solution)/shard_map/dot_general | solution.py:170
  26.7 0.1 collective-permute-start.5
  26.7 2.8 %collective-permute-done.7 = bf16[96,320]{0,1:T(8,128)(2,1)S(1)} collective-permute-done((bf16[96,320]{0,1:T(8,128)(2,1)S(1)}, bf16[96,320]{0,1:T(8,128)(2,1)S(1)}, u32[]{:S(2)}, u32[]{:S(2)}) %collective-permute-start.7) | collective-permute-done | bytes 61472 | tf_op jit(solution)/shard_map/ppermute | solution.py:25
  29.5 0.8 %fusion.41 = f32[128,320]{0,1:T(8,128)S(1)} fusion(bf16[96,320]{0,1:T(8,128)(2,1)S(1)} %collective-permute-done.7, s32[96]{0:T(128)} %collective-permute-done.6), kind=kOutput, calls=%fused_computation.81 | convolution fusion | flops 7876608 | bytes 225664 | tf_op jit(solution)/shard_map/dot_general | solution.py:170
  30.3 2.6 %collective-permute-done.5 = bf16[96,320]{0,1:T(8,128)(2,1)S(1)} collective-permute-done((bf16[96,320]{0,1:T(8,128)(2,1)S(1)}, bf16[96,320]{0,1:T(8,128)(2,1)S(1)}, u32[]{:S(2)}, u32[]{:S(2)}) %collective-permute-start.5) | collective-permute-done | bytes 61472 | tf_op jit(solution)/shard_map/ppermute | solution.py:25
  32.9 0.8 %fusion.40 = f32[128,320]{0,1:T(8,128)S(1)} fusion(bf16[96,320]{0,1:T(8,128)(2,1)S(1)} %collective-permute-done.5, s32[96]{0:T(128)} %collective-permute-done.4), kind=kOutput, calls=%fused_computation.80 | convolution fusion | flops 7876608 | bytes 225664 | tf_op jit(solution)/shard_map/dot_general | solution.py:170
  33.7 0.9 %fusion.13 = f32[128,320]{0,1:T(8,128)S(1)} fusion(f32[128,320]{0,1:T(8,128)S(1)} %fusion.41, f32[128,320]{0,1:T(8,128)S(1)} %fusion.40, f32[128,320]{0,1:T(8,128)S(1)} %convolution_add_fusion.3, bf16[96,320]{0,1:T(8,128)(2,1)S(1)} %collective-permute-done.3, s32[96]{0:T(128)} %collective-permute-done.2), kind=kOutput, calls=%fused_computation.29 | convolution fusion | flops 7999488 | bytes 717184 | tf_op jit(solution)/shard_map/dot_general | solution.py:170
  34.6 0.1 slice_bitcast_fusion.3
  34.7 6.6 %collective-permute-start.9 = (f32[1,5,8,8]{0,3,2,1:T(8,128)S(1)}, f32[1,5,8,8]{0,3,2,1:T(8,128)S(1)}, u32[]{:S(2)}, u32[]{:S(2)}) collective-permute-start(f32[1,5,8,8]{0,3,2,1:T(8,128)S(1)} %get-tuple-element.55), channel_id=1, source_target_pairs={{0,1},{1,2},{2,3},{3,4},{4,5},{5,6},{6,7},{7,8},{8,9},{9,10},{10,1... | collective-permute-start | bytes 3848 | tf_op jit(solution)/shard_map/ppermute | solution.py:33
  41.4 2.1 %collective-permute-start.8 = (f32[1,5,8,8]{0,3,2,1:T(8,128)S(1)}, f32[1,5,8,8]{0,3,2,1:T(8,128)S(1)}, u32[]{:S(2)}, u32[]{:S(2)}) collective-permute-start(f32[1,5,8,8]{0,3,2,1:T(8,128)S(1)} %get-tuple-element.56), channel_id=1, source_target_pairs={{1,0},{2,1},{3,2},{4,3},{5,4},{6,5},{7,6},{8,7},{9,8},{10,9},{11,1... | collective-permute-start | bytes 3848 | tf_op jit(solution)/shard_map/ppermute | solution.py:36
  43.5 0.1 fusion.16
  43.6 1.8 %collective-permute-done.9 = f32[1,5,8,8]{0,3,2,1:T(8,128)S(1)} collective-permute-done((f32[1,5,8,8]{0,3,2,1:T(8,128)S(1)}, f32[1,5,8,8]{0,3,2,1:T(8,128)S(1)}, u32[]{:S(2)}, u32[]{:S(2)}) %collective-permute-start.9) | collective-permute-done | bytes 1312 | tf_op jit(solution)/shard_map/ppermute | solution.py:33
  45.4 2.6 %collective-permute-done.8 = f32[1,5,8,8]{0,3,2,1:T(8,128)S(1)} collective-permute-done((f32[1,5,8,8]{0,3,2,1:T(8,128)S(1)}, f32[1,5,8,8]{0,3,2,1:T(8,128)S(1)}, u32[]{:S(2)}, u32[]{:S(2)}) %collective-permute-start.8) | collective-permute-done | bytes 1312 | tf_op jit(solution)/shard_map/ppermute | solution.py:36
  48.0 0.1 fusion.53
  48.1 0.1 fusion.18
  48.2 0.1 fusion.19
  48.4 1.8 %copy.56 = f32[128,5,8,8,8]{0,2,4,3,1:T(8,128)} copy(f32[128,5,8,8,8]{0,4,3,2,1:T(8,128)S(1)} %fusion.19) | data formatting | bytes 2621440 | tf_op jit(solution)/shard_map/scatter | solution.py:188
  50.2 0.4 copy.64
  50.6 0.3 copy-done.15
  50.8 3.1 %fusion.3 = f32[128,5,8,64]{0,2,3,1:T(8,128)S(1)} fusion(f32[128,5,8,64]{0,2,3,1:T(8,128)} %bitcast.154, f32[8,8,1,1]{1,0,3,2:T(8,128)S(1)} %copy-done.15, f32[128,8,64]{0,1,2:T(8,128)S(1)} %copy.58, f32[128,8,64]{0,1,2:T(8,128)S(1)} %copy.46), kind=kOutput, calls=%fused_computation.9 | convolution fusion | flops 32440320 | bytes 3145984 | tf_op jit(solution)/shard_map/ai,efip->efap/dot_general | solution.py:112
  54.0 1.2 %convolution_bitcast_fusion = f32[128,5,8,64]{0,2,3,1:T(8,128)S(1)} fusion(f32[128,5,8,64]{0,2,3,1:T(8,128)S(1)} %fusion.3, f32[8,8,1,1]{1,0,3,2:T(8,128)S(1)} %copy-done.15), kind=kOutput, calls=%fused_computation.6 | convolution fusion | flops 31457280 | bytes 2621696 | tf_op jit(solution)/shard_map/ai,efap->efip/dot_general | solution.py:124
  55.2 1.3 %copy.60 = f32[128,5,8,64]{0,3,2,1:T(8,128)} copy(f32[128,5,8,64]{0,2,3,1:T(8,128)S(1)} %convolution_bitcast_fusion) | data formatting | bytes 2621440 | tf_op jit(solution)/shard_map/ai,efap->efip/transpose | solution.py:124
  56.5 2.8 %copy.65 = f32[128,5,512]{2,0,1:T(8,128)} copy(f32[128,5,512]{0,2,1:T(8,128)} %bitcast.155) | data formatting | bytes 2621440 | tf_op jit(solution)/shard_map/reshape | solution.py:124
  59.4 5.7 %fusion.1 = f32[128,5,512]{2,0,1:T(8,128)S(1)} fusion(f32[128,5,512]{0,2,1:T(8,128)S(1)} %bitcast.152, f32[512,512,1]{1,0,2:T(8,128)} %constant.201, f32[128,5,512]{2,0,1:T(8,128)S(1)} %copy.64, f32[128,512]{1,0:T(8,128)S(1)} %copy-done.5, f32[128,512]{1,0:T(8,128)S(1)} %copy-done.3), kind=kOutput, calls=%fused_computation.5 | convolution fusion | flops 2014248960 | bytes 5505024 | tf_op jit(solution)/shard_map/efp,qp->efq/dot_general | solution.py:116
  65.1 2.2 %convolution_add_fusion.1 = f32[128,5,512]{2,0,1:T(8,128)S(1)} fusion(f32[128,5,512]{2,0,1:T(8,128)S(1)} %copy-done, f32[128,5,512]{2,0,1:T(8,128)S(1)} %fusion.1, f32[512,512,1]{1,0,2:T(8,128)S(1)} %copy-done.2), kind=kOutput, calls=%fused_computation.3 | convolution fusion | flops 2013593600 | bytes 4980736 | tf_op jit(solution)/shard_map/efq,qp->efp/dot_general | solution.py:128
  67.4 4.6 %fusion = f32[128,5,512]{2,0,1:T(8,128)S(1)} fusion(f32[128,5,512]{0,2,1:T(8,128)S(1)} %bitcast.153, f32[512,512,1]{1,0,2:T(8,128)S(1)} %copy-done.1, f32[128,5,512]{2,0,1:T(8,128)S(1)} %copy.64, f32[128,512]{1,0:T(8,128)S(1)} %copy-done.4, f32[128,512]{1,0:T(8,128)S(1)} %copy.67), kind=kOutput, calls=%fused_computation.2 | convolution fusion | flops 2014248960 | bytes 5505024 | tf_op jit(solution)/shard_map/efp,qp->efq/dot_general | solution.py:116
  72.0 3.3 %convolution_add_fusion = f32[128,5,512]{2,0,1:T(8,128)} fusion(f32[128,5,512]{2,0,1:T(8,128)S(1)} %convolution_add_fusion.1, f32[128,5,512]{2,0,1:T(8,128)S(1)} %fusion, f32[512,512,1]{1,0,2:T(8,128)S(1)} %copy-done.1), kind=kOutput, calls=%fused_computation | convolution fusion | flops 2013593600 | bytes 4980736 | tf_op jit(solution)/shard_map/efq,qp->efp/dot_general | solution.py:128
  (48 shorter events, 0.3 us)
Async XLA Ops:
  3.2 30.5 %collective-permute-start.2 = (s32[96]{0:T(128)}, s32[96]{0:T(128)}, u32[]{:S(2)}, u32[]{:S(2)}) collective-permute-start(s32[96]{0:T(128)} %get-tuple-element.67), channel_id=1, source_target_pairs={{4,0},{8,4},{12,8},{16,12},{20,16},{24,20},{28,24},{0,28},{5,1},{9... | collective-permute-start | bytes 1160 | tf_op jit(solution)/shard_map/ppermute | solution.py:25
  8.3 18.4 %collective-permute-start.6 = (s32[96]{0:T(128)}, s32[96]{0:T(128)}, u32[]{:S(2)}, u32[]{:S(2)}) collective-permute-start(s32[96]{0:T(128)} %get-tuple-element.68), channel_id=1, source_target_pairs={{24,0},{28,4},{0,8},{4,12},{8,16},{12,20},{16,24},{20,28},{25,1},{... | collective-permute-start | bytes 1160 | tf_op jit(solution)/shard_map/ppermute | solution.py:25
  8.3 22.0 %collective-permute-start.4 = (s32[96]{0:T(128)}, s32[96]{0:T(128)}, u32[]{:S(2)}, u32[]{:S(2)}) collective-permute-start(s32[96]{0:T(128)} %get-tuple-element.69), channel_id=1, source_target_pairs={{28,0},{0,4},{4,8},{8,12},{12,16},{16,20},{20,24},{24,28},{29,1},{... | collective-permute-start | bytes 1160 | tf_op jit(solution)/shard_map/ppermute | solution.py:25
  8.3 13.6 %collective-permute-start = (s32[96]{0:T(128)}, s32[96]{0:T(128)}, u32[]{:S(2)}, u32[]{:S(2)}) collective-permute-start(s32[96]{0:T(128)} %get-tuple-element.70), channel_id=1, source_target_pairs={{8,0},{12,4},{16,8},{20,12},{24,16},{28,20},{0,24},{4,28},{9,1},{1... | collective-permute-start | bytes 1160 | tf_op jit(solution)/shard_map/ppermute | solution.py:25
  12.9 1.8 %copy-start.14 = (f32[64,64,1]{0,1,2:T(8,128)S(1)}, f32[64,64,1]{0,1,2:T(8,128)}, u32[]{:S(2)}) copy-start(f32[64,64,1]{0,1,2:T(8,128)} %constant.192) | copy-start | bytes 49156
  12.9 2.1 %copy-start.13 = (f32[64,64,1]{0,1,2:T(8,128)S(1)}, f32[64,64,1]{0,1,2:T(8,128)}, u32[]{:S(2)}) copy-start(f32[64,64,1]{0,1,2:T(8,128)} %constant.193) | copy-start | bytes 49156
  12.9 2.4 %copy-start.12 = (f32[64,64,1]{0,1,2:T(8,128)S(1)}, f32[64,64,1]{0,1,2:T(8,128)}, u32[]{:S(2)}) copy-start(f32[64,64,1]{0,1,2:T(8,128)} %constant.194) | copy-start | bytes 49156
  14.6 1.0 %copy-start.11 = (f32[64,64,1]{0,1,2:T(8,128)S(1)}, f32[64,64,1]{0,1,2:T(8,128)}, u32[]{:S(2)}) copy-start(f32[64,64,1]{0,1,2:T(8,128)} %constant.195) | copy-start | bytes 49156
  14.6 1.3 %copy-start.10 = (f32[64,64,1]{0,1,2:T(8,128)S(1)}, f32[64,64,1]{0,1,2:T(8,128)}, u32[]{:S(2)}) copy-start(f32[64,64,1]{0,1,2:T(8,128)} %constant.196) | copy-start | bytes 49156
  14.7 1.6 %copy-start.9 = (f32[64,64,1]{0,1,2:T(8,128)S(1)}, f32[64,64,1]{0,1,2:T(8,128)}, u32[]{:S(2)}) copy-start(f32[64,64,1]{0,1,2:T(8,128)} %constant.197) | copy-start | bytes 49156
  15.0 1.6 %copy-start.8 = (f32[64,64,1]{0,1,2:T(8,128)S(1)}, f32[64,64,1]{0,1,2:T(8,128)}, u32[]{:S(2)}) copy-start(f32[64,64,1]{0,1,2:T(8,128)} %constant.198) | copy-start | bytes 49156
  15.3 1.6 %copy-start.7 = (f32[64,64,1]{0,1,2:T(8,128)S(1)}, f32[64,64,1]{0,1,2:T(8,128)}, u32[]{:S(2)}) copy-start(f32[64,64,1]{0,1,2:T(8,128)} %constant.199) | copy-start | bytes 49156
  16.3 1.4 %copy-start.16 = (s32[128,1]{0,1:T(1,128)S(1)}, s32[128,1]{0,1:T(1,128)}, u32[]{:S(2)}) copy-start(s32[128,1]{0,1:T(1,128)} %param.25) | copy-start | bytes 1540
  16.3 1.4 %copy-start.6 = (f32[128,3,512]{2,0,1:T(8,128)S(1)}, f32[128,3,512]{2,0,1:T(8,128)}, u32[]{:S(2)}) copy-start(f32[128,3,512]{2,0,1:T(8,128)} %param.20) | copy-start | bytes 2359300
  17.6 6.7 %collective-permute-start.1 = (bf16[96,320]{0,1:T(8,128)(2,1)S(1)}, bf16[96,320]{0,1:T(8,128)(2,1)S(1)}, u32[]{:S(2)}, u32[]{:S(2)}) collective-permute-start(bf16[96,320]{0,1:T(8,128)(2,1)S(1)} %get-tuple-element.66), channel_id=1, source_target_pairs={{8,0},{12,4},{16,8},{20,12},{24,16},{28,20},{0,24},{4,28},{9,1},{1... | collective-permute-start | bytes 184328 | tf_op jit(solution)/shard_map/ppermute | solution.py:25
  21.9 11.8 %collective-permute-start.3 = (bf16[96,320]{0,1:T(8,128)(2,1)S(1)}, bf16[96,320]{0,1:T(8,128)(2,1)S(1)}, u32[]{:S(2)}, u32[]{:S(2)}) collective-permute-start(bf16[96,320]{0,1:T(8,128)(2,1)S(1)} %get-tuple-element.63), channel_id=1, source_target_pairs={{4,0},{8,4},{12,8},{16,12},{20,16},{24,20},{28,24},{0,28},{5,1},{9... | collective-permute-start | bytes 184328 | tf_op jit(solution)/shard_map/ppermute | solution.py:25
  24.4 5.2 %collective-permute-start.7 = (bf16[96,320]{0,1:T(8,128)(2,1)S(1)}, bf16[96,320]{0,1:T(8,128)(2,1)S(1)}, u32[]{:S(2)}, u32[]{:S(2)}) collective-permute-start(bf16[96,320]{0,1:T(8,128)(2,1)S(1)} %get-tuple-element.64), channel_id=1, source_target_pairs={{24,0},{28,4},{0,8},{4,12},{8,16},{12,20},{16,24},{20,28},{25,1},{... | collective-permute-start | bytes 184328 | tf_op jit(solution)/shard_map/ppermute | solution.py:25
  26.7 6.2 %collective-permute-start.5 = (bf16[96,320]{0,1:T(8,128)(2,1)S(1)}, bf16[96,320]{0,1:T(8,128)(2,1)S(1)}, u32[]{:S(2)}, u32[]{:S(2)}) collective-permute-start(bf16[96,320]{0,1:T(8,128)(2,1)S(1)} %get-tuple-element.65), channel_id=1, source_target_pairs={{28,0},{0,4},{4,8},{8,12},{12,16},{16,20},{20,24},{24,28},{29,1},{... | collective-permute-start | bytes 184328 | tf_op jit(solution)/shard_map/ppermute | solution.py:25
  34.7 10.6 %collective-permute-start.9 = (f32[1,5,8,8]{0,3,2,1:T(8,128)S(1)}, f32[1,5,8,8]{0,3,2,1:T(8,128)S(1)}, u32[]{:S(2)}, u32[]{:S(2)}) collective-permute-start(f32[1,5,8,8]{0,3,2,1:T(8,128)S(1)} %get-tuple-element.55), channel_id=1, source_target_pairs={{0,1},{1,2},{2,3},{3,4},{4,5},{5,6},{6,7},{7,8},{8,9},{9,10},{10,1... | collective-permute-start | bytes 3848 | tf_op jit(solution)/shard_map/ppermute | solution.py:33
  41.4 6.6 %collective-permute-start.8 = (f32[1,5,8,8]{0,3,2,1:T(8,128)S(1)}, f32[1,5,8,8]{0,3,2,1:T(8,128)S(1)}, u32[]{:S(2)}, u32[]{:S(2)}) collective-permute-start(f32[1,5,8,8]{0,3,2,1:T(8,128)S(1)} %get-tuple-element.56), channel_id=1, source_target_pairs={{1,0},{2,1},{3,2},{4,3},{5,4},{6,5},{7,6},{8,7},{9,8},{10,9},{11,1... | collective-permute-start | bytes 3848 | tf_op jit(solution)/shard_map/ppermute | solution.py:36
  50.2 0.7 copy-start.15
  56.5 2.9 %copy-start.3 = (f32[128,512]{1,0:T(8,128)S(1)}, f32[128,512]{1,0:T(8,128)}, u32[]{:S(2)}) copy-start(f32[128,512]{1,0:T(8,128)} %copy.62) | copy-start | bytes 786436
  56.5 2.9 %copy-start.5 = (f32[128,512]{1,0:T(8,128)S(1)}, f32[128,512]{1,0:T(8,128)}, u32[]{:S(2)}) copy-start(f32[128,512]{1,0:T(8,128)} %get-tuple-element.62) | copy-start | bytes 786436
  59.4 5.7 %copy-start = (f32[128,5,512]{2,0,1:T(8,128)S(1)}, f32[128,5,512]{2,0,1:T(8,128)}, u32[]{:S(2)}) copy-start(f32[128,5,512]{2,0,1:T(8,128)} %copy.65) | copy-start | bytes 3932164
  59.4 5.7 %copy-start.2 = (f32[512,512,1]{1,0,2:T(8,128)S(1)}, f32[512,512,1]{1,0,2:T(8,128)}, u32[]{:S(2)}) copy-start(f32[512,512,1]{1,0,2:T(8,128)} %constant.201) | copy-start | bytes 3145732
  65.1 2.3 %copy-start.1 = (f32[512,512,1]{1,0,2:T(8,128)S(1)}, f32[512,512,1]{1,0,2:T(8,128)}, u32[]{:S(2)}) copy-start(f32[512,512,1]{1,0,2:T(8,128)} %constant.202) | copy-start | bytes 3145732
  65.1 2.3 %copy-start.4 = (f32[128,512]{1,0:T(8,128)S(1)}, f32[128,512]{1,0:T(8,128)}, u32[]{:S(2)}) copy-start(f32[128,512]{1,0:T(8,128)} %get-tuple-element.60) | copy-start | bytes 786436
where the time goes:
time: 75.7 us; the launch traced here: 75.3 us
  matrix products  26.4 us (35%)
  starting transfers between devices  21 us (28%)
  local copies, waits for them, and re-layouts  13 us (17%)
  waiting for transfers between devices  9.78 us (13%)
  other arithmetic  4.51 us (6%)
    ppermute x8, starting transfers between devices, passed_along(): return lax.ppermute(block, axis, route)  12.3 us
    dot_general x2, matrix products, derive(): jnp.einsum('efp,qp->efq', field, kron_mat, precision=lax.Precision.HIGHEST)  10.3 us
    ppermute x1, starting transfers between devices, extended(): lax.ppermute(lax.slice_in_dim(block, block.shape[dim] - width, None, axis...  6.62 us
    dot_general x2, matrix products, derive_back(): jnp.einsum('efq,qp->efp', field, kron_mat, precision=lax.Precision.HIGHEST)  5.59 us
    ppermute x8, waiting for transfers between devices, passed_along(): return lax.ppermute(block, axis, route)  5.37 us
    dot_general x5, matrix products, absorb(): return total + jnp.dot(hit, faces, preferred_element_type=jnp.float32)  3.54 us
    dot_general x1, matrix products, derive(): jnp.einsum('ai,efip->efap', dmat, cube, precision=lax.Precision.HIGHEST)  3.11 us
    reshape x1, local copies, waits for them, and re-layouts, derive_back(): jnp.einsum('ai,efap->efip', dmat, cube, precision=lax.Precision.HIGHEST)  2.84 us
  transfers between devices with their start and end apart: 10, of which 4 were waited for; matrix products, arithmetic and copies ran while one was open for 17% of the time, Pallas kernels for 0%

commit v1 on v0

v1 whole, which is shorter than its diff:
```python
import jax
import jax.numpy as jnp
import ml_dtypes
import numpy as np
from jax import lax
from jax.experimental import pallas as pl
from jax.experimental.pallas import tpu as pltpu
from jax.sharding import PartitionSpec as P

gll_nodes = np.array(
    [
        -1.0,
        -0.8717401485096066,
        -0.5917001814331423,
        -0.2092992179024789,
        0.2092992179024789,
        0.5917001814331423,
        0.8717401485096066,
        1.0,
    ]
)
viscosity = 0.005
F32, BF16 = jnp.float32, jnp.bfloat16
E = 128
ANY = pl.BlockSpec(memory_space=pl.ANY)
VM = pl.BlockSpec(memory_space=pltpu.VMEM)
SM = pl.BlockSpec(memory_space=pltpu.SMEM)
LIMIT = 32 * 1024 * 1024


def legendre_seven(points):
    prev = np.ones(points.shape)
    curr = np.array(points)
    for order in range(1, 7):
        nxt = ((2 * order + 1) * points * curr - order * prev) / (order + 1)
        prev, curr = (curr, nxt)
    return curr


def diff_matrix():
    values = legendre_seven(gll_nodes)
    result_mat = np.zeros((8, 8))
    for row in range(8):
        for col in range(8):
            if row != col:
                result_mat[row, col] = values[row] / (
                    values[col] * (gll_nodes[row] - gll_nodes[col])
                )
    result_mat[0, 0] = -14.0
    result_mat[7, 7] = 14.0
    return result_mat


def lagrange_at(points):
    basis = np.ones((8, 8))
    for row in range(8):
        for col in range(8):
            for other in range(8):
                if other != col:
                    basis[row, col] *= (points[row] - gll_nodes[other]) / (
                        gll_nodes[col] - gll_nodes[other]
                    )
    return basis


def face_tables():
    halves = [lagrange_at((gll_nodes - 1.0) / 2.0), lagrange_at((gll_nodes + 1.0) / 2.0)]
    perm_mat = np.zeros((64, 64))
    for col in range(64):
        perm_mat[col % 8 * 8 + col // 8, col] = 1.0
    tables = []
    for code in range(8):
        mat = np.kron(halves[code % 2], halves[code // 2 % 2])
        if code >= 4:
            mat = mat @ perm_mat
        tables.append(mat)
    return np.stack(tables)


def two_parts(mat):
    high = mat.astype(ml_dtypes.bfloat16)
    low = (mat - high.astype(np.float64)).astype(ml_dtypes.bfloat16)
    return high, low


def constants():
    dmat = diff_matrix()
    eye = np.eye(8)
    along_j = np.kron(np.eye(2), np.kron(dmat, eye))
    along_k = np.kron(np.eye(16), dmat)
    along_i = along_j

    def forward(first, second):
        fh, fl = two_parts(viscosity * first.T)
        sh, sl = two_parts(viscosity * second.T)
        top = np.concatenate([fh, sh], 1)
        return np.concatenate([top, top], 0), np.concatenate([fl, sl], 1)

    def backward(first, second):
        fh, fl = two_parts(first)
        sh, sl = two_parts(second)
        return (
            np.concatenate([np.concatenate([fh, fl], 1), np.concatenate([sh, sl], 1)], 0),
            np.concatenate([fh, sh], 0),
        )

    def split_parity(mat):
        vectors = []
        for sign in (1.0, -1.0):
            small = (mat[:4, :4] + sign * mat[:4, ::-1][:, :4]) / 2
            for c in range(2):
                for other in range(2):
                    for swap in (0, 1):
                        vectors.append(
                            np.concatenate(
                                [
                                    np.full(64, small[2 * c + h, 2 * other + (h ^ swap)])
                                    for h in range(2)
                                ]
                            )
                        )
        return np.stack(vectors)

    coef = np.concatenate([split_parity(viscosity * dmat), split_parity(dmat.T)], 0)
    column = np.tile(np.repeat(viscosity * dmat[:, 0], 8), 2)[None]
    coef = np.concatenate([coef, column, np.zeros((7, 128))], 0).astype(np.float32)

    tables = face_tables()
    fold = np.zeros((256, 512), ml_dtypes.bfloat16)
    for code in range(8):
        high, low = two_parts(tables[code])
        for i in range(8):
            for k in range(8):
                c, h = i // 2, i % 2
                spot = (56 + 64 * h + 16 * c + k) % 128
                cols = slice(64 * code, 64 * code + 64)
                fold[spot, cols] = high[8 * i + k]
                fold[(spot + 8) % 128, cols] = high[8 * i + k]
                fold[128 + spot, cols] = low[8 * i + k]

    spread = np.zeros((64, 512))
    place = np.zeros((64, 512))
    for i in range(8):
        for k in range(8):
            place[8 * i + k, 64 * i + k] = 1.0
            for j in range(8):
                spread[8 * i + k, 64 * i + 8 * j + k] = 1.0
    zero = np.zeros((64, 512))

    def pair(mat):
        one = np.concatenate(
            [np.concatenate([mat, zero], 1), np.concatenate([zero, mat], 1)], 0
        )
        return np.concatenate([one, one], 0).astype(ml_dtypes.bfloat16)

    return {
        "fold": fold,
        "forward": forward(along_j, along_k),
        "backward": backward(along_j, along_k),
        "face_forward": forward(along_i, along_k),
        "face_backward": backward(along_i, along_k),
        "spread": pair(spread),
        "place": pair(place),
        "coef": coef,
    }


def iota(dim, shape=(E, 128)):
    return lax.broadcasted_iota(jnp.int32, shape, dim)


def down(row):
    spots = jnp.where(iota(0) == iota(1), row, 0).astype(F32).astype(BF16)
    return jnp.dot(spots, jnp.ones((E, 128), BF16), preferred_element_type=F32)


def dot(a, b):
    return jnp.dot(a, b, preferred_element_type=F32)


def parts_of(x):
    high = x.astype(BF16)
    return high, (x - high.astype(F32)).astype(BF16)


def edge_kernel(hang_ref, low_ref, high_ref, low_out, high_out):
    lane = iota(1, (1, 128)) % 64
    low_out[...] = jnp.zeros((8, 128), F32)
    high_out[...] = jnp.zeros((8, 128), F32)
    low_keep = jnp.where(lane >= 56, 1.0 - hang_ref[0, 0].astype(F32), 1.0)
    high_keep = jnp.where(lane >= 56, 1.0 - hang_ref[0, E - 1].astype(F32), 1.0)
    for f in range(5):
        low_out[f : f + 1] = pltpu.roll(low_ref[f, 0:1] * low_keep, 64, 1)
        high_out[f : f + 1] = pltpu.roll(high_ref[f, 7:8] * high_keep, 64, 1)


def edges_of(adjoint, hang):
    return pl.pallas_call(
        edge_kernel,
        grid=(1,),
        out_shape=[jax.ShapeDtypeStruct((8, 128), F32)] * 2,
        in_specs=[
            SM,
            pl.BlockSpec((5, 8, 128), lambda g: (0, 0, 0)),
            pl.BlockSpec((5, 8, 128), lambda g: (0, E // 8 - 1, 3)),
        ],
        out_specs=[pl.BlockSpec((8, 128), lambda g: (0, 0))] * 2,
        name="edges",
    )(hang, adjoint, adjoint)


def fold_kernel(peers, adj_hbm, route, target, code, hang, fold, *refs):
    outs, own, x, sems = refs[:4], refs[4], refs[5], refs[6]
    copies = [pltpu.make_async_copy(adj_hbm.at[f], x.at[f], sems.at[f]) for f in range(5)]
    for copy in copies:
        copy.start()
    slot = lax.rem(route[...] - lax.axis_index("dom") + 2 + peers, peers)
    spot = slot * E + target[...]
    hit = (iota(0, (5 * E, E)) == spot).astype(F32).astype(BF16)
    lane = iota(1)
    marked = down(jnp.where(hang[...] == 1, code[...], -2)) - (lane // 64).astype(F32)
    odd = lane % 16 >= 8
    group = (lane // 16 + 1) % 4
    faces = []
    for f in range(5):
        copies[f].wait()
        packed = jnp.zeros((E, 128), F32)
        for c in range(4):
            moved = x[f, :, 128 * c : 128 * c + 128]
            if c:
                moved = pltpu.roll(moved, 16 * c, 1)
            packed = jnp.where(odd & (group == c), moved, packed)
        high = packed.astype(BF16)
        high_f = high.astype(F32)
        both = jnp.where(odd, high_f, pltpu.roll(packed - high_f, 8, 1)).astype(BF16)
        mapped = dot(jnp.concatenate([both, high], 1), fold[...])
        total = jnp.zeros((E, 128), F32)
        for q in range(4):
            total = total + jnp.where(
                marked == 2.0 * q, mapped[:, 128 * q : 128 * q + 128], 0.0
            )
        faces.append(total + pltpu.roll(total, 64, 1))
    left = lane < 64
    f01 = jnp.where(left, faces[0], faces[1]).astype(BF16)
    f23 = jnp.where(left, faces[2], faces[3]).astype(BF16)
    f4 = faces[4].astype(BF16)
    rhs = jnp.concatenate([f01, f23, f4], 1)
    for o in range(5):
        ref = (outs[0], outs[1], own, outs[2], outs[3])[o]
        sums = dot(hit[o * E : o * E + E], rhs)
        ref[0:128] = sums[:, 0:128].astype(ref.dtype)
        ref[128:256] = sums[:, 128:256].astype(ref.dtype)
        last = jnp.where(left[:64], sums[:64, 256:384], sums[64:, 256:384])
        ref[256:320] = last.astype(ref.dtype)


def folded_of(adjoint, route, target, code, hang, fold, peers):
    def body(*refs):
        fold_kernel(peers, *refs)

    return pl.pallas_call(
        body,
        out_shape=[jax.ShapeDtypeStruct((320, 128), BF16)] * 4
        + [jax.ShapeDtypeStruct((320, 128), F32)],
        in_specs=[ANY] + [VM] * 5,
        out_specs=[VM] * 5,
        scratch_shapes=[pltpu.VMEM((5, E, 512), F32), pltpu.SemaphoreType.DMA((5,))],
        compiler_params=pltpu.CompilerParams(vmem_limit_bytes=LIMIT),
        name="fold",
    )(adjoint, route, target, code, hang, fold)


def swap(x):
    return pltpu.roll(x, 64, 1)


def along_first(x, coef, base):
    r3, r2 = swap(x[3]), swap(x[2])
    parity = ((x[0] + r3, x[1] + r2), (x[0] - r3, x[1] - r2))
    sums = []
    for s in range(2):
        kept = (parity[s][0], swap(parity[s][0]), parity[s][1], swap(parity[s][1]))
        for c in range(2):
            at = base + 8 * s + 4 * c
            total = coef[at : at + 1] * kept[0]
            for n in range(1, 4):
                total = total + coef[at + n : at + n + 1] * kept[n]
            sums.append(total)
    p0, p1, q0, q1 = sums
    return [p0 + q0, p1 + q1, swap(q1 - p1), swap(q0 - p0)]


def main_kernel(
    adj_hbm, met_hbm, vel_hbm, hang, before, after, wf1, wf2, wb1, wb2, coef,
    out, q_out, plane_out, x_ref, met, vel, sems,
):
    loads = [
        pltpu.make_async_copy(met_hbm, met, sems.at[0]),
        pltpu.make_async_copy(vel_hbm, vel, sems.at[1]),
        pltpu.make_async_copy(adj_hbm, x_ref, sems.at[2]),
    ]
    for copy in loads:
        copy.start()
    lane, row = iota(1), iota(0)
    keep = jnp.where(lane % 64 >= 56, 1.0 - down(hang[...]), 1.0)
    left = lane < 64
    for copy in loads:
        copy.wait()

    for c in range(4):
        at = slice(128 * c, 128 * c + 128)
        w = met[1, :, at] * coef[32:33] + jnp.where(lane % 64 < 8, vel[1, :, at], 0.0)
        high, low = parts_of(w)
        wide = dot(high, wb1[0:128])
        q_out[:, at] = wide[:, :128] + wide[:, 128:] + dot(low, wb2[0:128])

    for n, (ref, d) in enumerate(((met, 0), (met, 2), (vel, 0), (vel, 2))):
        packed = jnp.zeros((E, 128), F32)
        for c in range(4):
            moved = ref[d, :, 128 * c : 128 * c + 128]
            if c:
                moved = pltpu.roll(moved, 16 * c, 1)
            packed = jnp.where((lane // 16) % 4 == c, moved, packed)
        even = jnp.where(left, packed, swap(packed))
        other = jnp.where(left, swap(packed), packed)
        plane_out[n] = jnp.where(lane % 16 < 8, even, pltpu.roll(other, 8, 1))

    def field(f, carry):
        x = [x_ref[f, :, 128 * c : 128 * c + 128] * keep for c in range(4)]
        low_faces = pltpu.roll(swap(x[0]), E - 1, 0)
        high_faces = pltpu.roll(swap(x[3]), 1, 0)
        low_faces = jnp.where(row == E - 1, after[pl.ds(f, 1)], low_faces)
        high_faces = jnp.where(row == 0, before[pl.ds(f, 1)], high_faces)
        x[0] = x[0] + jnp.where(left, high_faces, 0.0)
        x[3] = x[3] + jnp.where(left, 0.0, low_faces)
        g0 = along_first(x, coef, 0)
        inner0 = []
        totals = []
        for c in range(4):
            at = slice(128 * c, 128 * c + 128)
            high, low = parts_of(x[c])
            g = dot(jnp.concatenate([high, low], 1), wf1[...]) + dot(high, wf2[...])
            inner0.append(met[0, :, at] * g0[c] + vel[0, :, at] * x[c])
            in1 = met[1, :, at] * g[:, :128] + vel[1, :, at] * x[c]
            in2 = met[2, :, at] * g[:, 128:] + vel[2, :, at] * x[c]
            high1, low1 = parts_of(in1)
            high2, low2 = parts_of(in2)
            wide = dot(jnp.concatenate([high1, high2], 1), wb1[...])
            totals.append(
                wide[:, :128]
                + wide[:, 128:]
                + dot(jnp.concatenate([low1, low2], 1), wb2[...])
            )
        back = along_first(inner0, coef, 16)
        for c in range(4):
            out[f, :, 128 * c : 128 * c + 128] = totals[c] + back[c]
        return carry

    lax.fori_loop(0, 5, field, 0)


def main_of(adjoint, metric, velocity, hang, before, after, tables):
    return pl.pallas_call(
        main_kernel,
        out_shape=[
            jax.ShapeDtypeStruct((5, E, 512), F32),
            jax.ShapeDtypeStruct((E, 512), F32),
            jax.ShapeDtypeStruct((4, E, 128), F32),
        ],
        in_specs=[ANY] * 3 + [VM] * 8,
        out_specs=[VM] * 3,
        scratch_shapes=[
            pltpu.VMEM((5, E, 512), F32),
            pltpu.VMEM((3, E, 512), F32),
            pltpu.VMEM((3, E, 512), F32),
            pltpu.SemaphoreType.DMA((3,)),
        ],
        compiler_params=pltpu.CompilerParams(vmem_limit_bytes=LIMIT),
        cost_estimate=pl.CostEstimate(
            flops=4_000_000_000, bytes_accessed=6_000_000, transcendentals=0
        ),
        name="inner",
    )(
        adjoint, metric, velocity, hang, before, after,
        *tables["forward"], *tables["backward"], tables["coef"],
    )


def line_kernel(a, b, own, c, d, low_out, high_out):
    def rows(start):
        return sum(
            ref[start : start + 16].astype(F32) for ref in (a, b, own, c, d)
        )

    low_out[...] = jnp.zeros((8, 128), F32)
    high_out[...] = jnp.zeros((8, 128), F32)
    for n, (first, last) in enumerate(((0, 112), (128, 240), (256, 304))):
        low_out[n : n + 1] = pltpu.roll(rows(first)[0:1], 56, 1)
        line = rows(last)[15:16]
        high_out[n : n + 1] = pltpu.roll(swap(line) if n == 2 else line, 72, 1)


def lines_of(parts):
    return pl.pallas_call(
        line_kernel,
        out_shape=[jax.ShapeDtypeStruct((8, 128), F32)] * 2,
        in_specs=[VM] * 5,
        out_specs=[VM] * 2,
        name="lines",
    )(*parts)


def post_kernel(
    a, b, own, c, d, before, after, base, q_ref, plane, wf1, wf2, wb1, wb2,
    spread, place, out_hbm, out, sems,
):
    lane, row = iota(1), iota(0)
    left = lane < 64
    refs = (a, b, own, c, d)
    copies = [pltpu.make_async_copy(out.at[f], out_hbm.at[f], sems.at[f]) for f in range(5)]
    for n in range(3):
        rows = slice(128 * n, min(128 * n + 128, 320))
        m = sum(ref[rows].astype(F32) for ref in refs)
        if n == 2:
            m = jnp.concatenate([m, swap(m)], 0)
        low_lines = pltpu.roll(pltpu.roll(m, 56, 1), E - 1, 0)
        high_lines = pltpu.roll(pltpu.roll(m, 72, 1), 1, 0)
        low_lines = jnp.where(row == E - 1, after[n : n + 1], low_lines)
        high_lines = jnp.where(row == 0, before[n : n + 1], high_lines)
        y = m + jnp.where(lane % 64 < 8, high_lines, 0.0)
        y = y + jnp.where(lane % 64 >= 56, low_lines, 0.0)
        high, low = parts_of(y)
        y_parts = jnp.concatenate([high, low], 1)
        g = dot(y_parts, wf1[...]) + dot(high, wf2[...])
        in0 = plane[0] * g[:, :128] + plane[2] * y
        in2 = plane[1] * g[:, 128:] + plane[3] * y
        high0, low0 = parts_of(in0)
        high2, low2 = parts_of(in2)
        wide = dot(jnp.concatenate([high0, high2], 1), wb1[...])
        r = wide[:, :128] + wide[:, 128:] + dot(jnp.concatenate([low0, low2], 1), wb2[...])
        r_parts = jnp.concatenate(parts_of(r), 1)
        for f in range(2 * n, min(2 * n + 2, 5)):
            for c_at in range(4):
                at = slice(128 * c_at, 128 * c_at + 128)
                cols = slice(512 * (f - 2 * n) + 128 * c_at, 512 * (f - 2 * n) + 128 * c_at + 128)
                out[f, :, at] = (
                    base[f, :, at]
                    + q_ref[:, at] * dot(y_parts, spread[:, cols])
                    + dot(r_parts, place[:, cols])
                )
            copies[f].start()
    for copy in copies:
        copy.wait()


def post_of(parts, before, after, base, q, plane, tables):
    return pl.pallas_call(
        post_kernel,
        out_shape=jax.ShapeDtypeStruct((5, E, 512), F32),
        in_specs=[VM] * 16,
        out_specs=ANY,
        scratch_shapes=[pltpu.VMEM((5, E, 512), F32), pltpu.SemaphoreType.DMA((5,))],
        compiler_params=pltpu.CompilerParams(vmem_limit_bytes=LIMIT),
        name="outer",
    )(
        *parts, before, after, base, q, plane,
        *tables["face_forward"], *tables["face_backward"],
        tables["spread"], tables["place"],
    )


def both_ways(low, high):
    axes = ("dom", "sub")
    count = lax.axis_size(axes)
    forward = [(i, i + 1) for i in range(count - 1)]
    backward = [(i + 1, i) for i in range(count - 1)]
    return lax.ppermute(high, axes, forward), lax.ppermute(low, axes, backward)


def shards(adjoint_field, metric, velocity, mortar_route, mortar_element, face_code, hanging):
    tables = constants()
    peers = lax.axis_size("dom")
    adjoint = jnp.transpose(adjoint_field, (1, 0, 2))
    met = jnp.transpose(metric, (1, 0, 2))
    vel = jnp.transpose(velocity, (1, 0, 2))
    route, target, code, hang = (
        x.reshape(1, E) for x in (mortar_route, mortar_element, face_code, hanging)
    )
    low, high = edges_of(adjoint, hang)
    before, after = both_ways(low, high)
    *sends, own = folded_of(adjoint, route, target, code, hang, tables["fold"], peers)
    got = []
    for send, offset in zip(sends, (-2, -1, 1, 2)):
        pairs = [(i, (i + offset) % peers) for i in range(peers)]
        got.append(lax.ppermute(send, "dom", pairs))
    base, q, plane = main_of(adjoint, met, vel, hang, before, after, tables)
    parts = (got[0], got[1], own, got[2], got[3])
    line_before, line_after = both_ways(*lines_of(parts))
    result = post_of(parts, line_before, line_after, base, q, plane, tables)
    return jnp.transpose(result, (1, 0, 2))


def solution(mesh):
    block = P(("dom", "sub"), None, None)
    flat = P(("dom", "sub"), None)
    return jax.shard_map(
        shards,
        mesh=mesh,
        in_specs=(block, block, block, flat, flat, flat, flat),
        out_specs=block,
        check_vma=False,
    )
```

time: 75.7 us -> 41.5 us (0.55)
  the two profiles are of different devices: /device:TPU:1 before, /device:TPU:24 now
where the time goes in v1:
time: 41.5 us; the launch traced here: 41.1 us
  starting transfers between devices  20.6 us (50%)
  Pallas kernels  12.8 us (31%)
  local copies, waits for them, and re-layouts  7.38 us (18%)
    ppermute x2, starting transfers between devices, both_ways(): lax.ppermute(low, axes, backward)  10.9 us
    unnamed x54, local copies, waits for them, and re-layouts  7.38 us
    ppermute x4, starting transfers between devices, shards(): got.append(lax.ppermute(send, 'dom', pairs))  5.9 us
    pallas_call x1, Pallas kernels, main_of(): pl.pallas_call(main_kernel, out_shape=[jax.ShapeDtypeStruct((5, E, 512),...  4.73 us
    ppermute x2, starting transfers between devices, both_ways(): lax.ppermute(high, axes, forward)  3.82 us
    pallas_call x1, Pallas kernels, folded_of(): pl.pallas_call(body, out_shape=[jax.ShapeDtypeStruct((320, 128), BF16)] *...  2.49 us
    pallas_call x1, Pallas kernels, post_of(): pl.pallas_call(post_kernel, out_shape=jax.ShapeDtypeStruct((5, E, 512), F...  2.31 us
    pallas_call x1, Pallas kernels, lines_of(): pl.pallas_call(line_kernel, out_shape=[jax.ShapeDtypeStruct((8, 128), F32...  1.82 us
  transfers between devices with their start and end apart: 8, of which 0 were waited for; matrix products, arithmetic and copies ran while one was open for 0% of the time, Pallas kernels for 19%

profile of v1, /device:TPU:24, one launch (start us, length us, event | category | flops | bytes accessed | tf_op | source)
XLA Modules:
  0.0 41.1 jit_solution(15265142913288915605)
XLA Ops:
  0.0 0.0 copy-start
  0.0 1.3 %copy-done = f32[128,5,512]{2,0,1:T(8,128)S(1)} copy-done((f32[128,5,512]{2,0,1:T(8,128)S(1)}, f32[128,5,512]{2,0,1:T(8,128)}, u32[]{:S(2)}) %copy-start) | copy-done | bytes 1310744
  1.3 0.0 copy-start.14
  1.3 0.9 %copy-done.14 = bf16[256,512]{1,0:T(8,128)(2,1)S(1)} copy-done((bf16[256,512]{1,0:T(8,128)(2,1)S(1)}, bf16[256,512]{1,0:T(8,128)(2,1)}, u32[]{:S(2)}) %copy-start.14) | copy-done | bytes 262168
  2.3 0.0 copy-start.19
  2.3 0.7 %copy-done.19 = s32[128,1]{0,1:T(1,128)S(1)} copy-done((s32[128,1]{0,1:T(1,128)S(1)}, s32[128,1]{0,1:T(1,128)}, u32[]{:S(2)}) %copy-start.19) | copy-done | bytes 536
  2.9 0.7 %copy-done.21 = s32[128,1]{0,1:T(1,128)S(1)} copy-done((s32[128,1]{0,1:T(1,128)S(1)}, s32[128,1]{0,1:T(1,128)}, u32[]{:S(2)}) %copy-start.21) | copy-done | bytes 536
  3.6 0.7 %copy-done.22 = s32[128,1]{0,1:T(1,128)S(1)} copy-done((s32[128,1]{0,1:T(1,128)S(1)}, s32[128,1]{0,1:T(1,128)}, u32[]{:S(2)}) %copy-start.22) | copy-done | bytes 536
  4.2 0.7 %copy-done.23 = s32[128,1]{0,1:T(1,128)S(1)} copy-done((s32[128,1]{0,1:T(1,128)S(1)}, s32[128,1]{0,1:T(1,128)}, u32[]{:S(2)}) %copy-start.23) | copy-done | bytes 536
  4.9 2.5 %fold.1 = (bf16[320,128]{1,0:T(8,128)(2,1)S(1)}, bf16[320,128]{1,0:T(8,128)(2,1)S(1)}, bf16[320,128]{1,0:T(8,128)(2,1)S(1)}, bf16[320,128]{1,0:T(8,128)(2,1)S(1)}, f32[320,128]{1,0:T(8,128)S(1)}) custom-call(f32[5,128,512]{2,1,0:T(8,128)S(1)} %bitcast.10, s32[1,128]{1,0:T(1,128)S(1)} %bitcast.15, s32[1,128]{1,0:T(1,128)S(1)} %bitcast.16, ...), custom_call_target="tpu_custom_call" | custom-call | tf_op jit(solution)/shard_map/fold/pallas_call | solution.py:261
  7.4 0.0 copy-start.2
  7.4 0.7 %copy-done.2 = f32[320,128]{1,0:T(8,128)} copy-done((f32[320,128]{1,0:T(8,128)}, f32[320,128]{1,0:T(8,128)S(1)}, u32[]{:S(2)}) %copy-start.2) | copy-done | bytes 163864
  8.1 0.4 %collective-permute-start = (bf16[320,128]{1,0:T(8,128)(2,1)S(1)}, bf16[320,128]{1,0:T(8,128)(2,1)S(1)}, u32[]{:S(2)}, u32[]{:S(2)}) collective-permute-start(bf16[320,128]{1,0:T(8,128)(2,1)S(1)} %get-tuple-element.17), channel_id=1, source_target_pairs={{0,24},{4,28},{8,0},{12,4},{16,8},{20,12},{24,16},{28,20},{1,25},{... | collective-permute-start | bytes 245768 | tf_op jit(solution)/shard_map/ppermute | solution.py:495
  8.5 1.4 %collective-permute-start.1 = (bf16[320,128]{1,0:T(8,128)(2,1)S(1)}, bf16[320,128]{1,0:T(8,128)(2,1)S(1)}, u32[]{:S(2)}, u32[]{:S(2)}) collective-permute-start(bf16[320,128]{1,0:T(8,128)(2,1)S(1)} %get-tuple-element.18), channel_id=1, source_target_pairs={{0,28},{4,0},{8,4},{12,8},{16,12},{20,16},{24,20},{28,24},{1,29},{... | collective-permute-start | bytes 245768 | tf_op jit(solution)/shard_map/ppermute | solution.py:495
  9.9 0.6 %collective-permute-start.2 = (bf16[320,128]{1,0:T(8,128)(2,1)S(1)}, bf16[320,128]{1,0:T(8,128)(2,1)S(1)}, u32[]{:S(2)}, u32[]{:S(2)}) collective-permute-start(bf16[320,128]{1,0:T(8,128)(2,1)S(1)} %get-tuple-element.20), channel_id=1, source_target_pairs={{0,4},{4,8},{8,12},{12,16},{16,20},{20,24},{24,28},{28,0},{1,5},{5... | collective-permute-start | bytes 245768 | tf_op jit(solution)/shard_map/ppermute | solution.py:495
  10.5 0.0 copy-start.18
  10.6 0.0 copy-start.20
  10.6 0.0 copy-start.24
  10.6 0.0 copy-start.26
  10.6 3.4 %collective-permute-start.3 = (bf16[320,128]{1,0:T(8,128)(2,1)S(1)}, bf16[320,128]{1,0:T(8,128)(2,1)S(1)}, u32[]{:S(2)}, u32[]{:S(2)}) collective-permute-start(bf16[320,128]{1,0:T(8,128)(2,1)S(1)} %get-tuple-element.21), channel_id=1, source_target_pairs={{0,8},{4,12},{8,16},{12,20},{16,24},{20,28},{24,0},{28,4},{1,9},{5... | collective-permute-start | bytes 245768 | tf_op jit(solution)/shard_map/ppermute | solution.py:495
  14.0 1.4 %edges.1 = (f32[8,128]{1,0:T(8,128)}, f32[8,128]{1,0:T(8,128)}) custom-call(s32[1,128]{1,0:T(1,128)} %bitcast.12, f32[5,128,512]{2,1,0:T(8,128)} %bitcast.8, f32[5,128,512]{2,1,0:T(8,128)} %bitcast.9), custom_call_target="tpu_custom_call" | custom-call | tf_op jit(solution)/shard_map/edges/pallas_call | solution.py:198
  15.5 1.9 %collective-permute-start.6 = (f32[8,128]{1,0:T(8,128)}, f32[8,128]{1,0:T(8,128)S(1)}, u32[]{:S(2)}, u32[]{:S(2)}) collective-permute-start(f32[8,128]{1,0:T(8,128)} %get-tuple-element.24), channel_id=1, source_target_pairs={{0,1},{1,2},{2,3},{3,4},{4,5},{5,6},{6,7},{7,8},{8,9},{9,10},{10,1... | collective-permute-start | bytes 12296 | tf_op jit(solution)/shard_map/ppermute | solution.py:477
  17.4 0.0 collective-permute-done.a
  17.4 0.0 copy-start.6
  17.4 5.4 %collective-permute-start.7 = (f32[8,128]{1,0:T(8,128)}, f32[8,128]{1,0:T(8,128)S(1)}, u32[]{:S(2)}, u32[]{:S(2)}) collective-permute-start(f32[8,128]{1,0:T(8,128)} %get-tuple-element.25), channel_id=1, source_target_pairs={{1,0},{2,1},{3,2},{4,3},{5,4},{6,5},{7,6},{8,7},{9,8},{10,9},{11,1... | collective-permute-start | bytes 12296 | tf_op jit(solution)/shard_map/ppermute | solution.py:477
  22.8 0.0 collective-permute-done.1.b
  22.8 0.0 copy-start.8
  22.9 0.0 collective-permute-done.2.c
  22.9 0.0 copy-start.10
  22.9 0.0 collective-permute-done.3.d
  22.9 0.0 copy-start.12
  22.9 0.0 copy-done.6
  22.9 0.6 %copy-done.8 = bf16[320,128]{1,0:T(8,128)(2,1)} copy-done((bf16[320,128]{1,0:T(8,128)(2,1)}, bf16[320,128]{1,0:T(8,128)(2,1)S(1)}, u32[]{:S(2)}) %copy-start.8) | copy-done | bytes 81944
  23.5 0.0 copy-done.10
  23.5 0.0 copy-done.12
  23.5 1.8 %lines.1 = (f32[8,128]{1,0:T(8,128)}, f32[8,128]{1,0:T(8,128)}) custom-call(bf16[320,128]{1,0:T(8,128)(2,1)} %copy-done.6, bf16[320,128]{1,0:T(8,128)(2,1)} %copy-done.8, f32[320,128]{1,0:T(8,128)} %copy-done.2, bf16[320,128]{1,0:T(8,128)(2,1)} %copy-done.10, bf16[320,128]{1,0:T(8,128)(2,1)} %copy-done.12), custom_call_target="tpu_custom_call" | custom-call | tf_op jit(solution)/shard_map/lines/pallas_call | solution.py:404
  25.4 1.9 %collective-permute-start.4 = (f32[8,128]{1,0:T(8,128)}, f32[8,128]{1,0:T(8,128)S(1)}, u32[]{:S(2)}, u32[]{:S(2)}) collective-permute-start(f32[8,128]{1,0:T(8,128)} %get-tuple-element.22), channel_id=1, source_target_pairs={{0,1},{1,2},{2,3},{3,4},{4,5},{5,6},{6,7},{7,8},{8,9},{9,10},{10,1... | collective-permute-start | bytes 12296 | tf_op jit(solution)/shard_map/ppermute | solution.py:477
  27.3 5.4 %collective-permute-start.5 = (f32[8,128]{1,0:T(8,128)}, f32[8,128]{1,0:T(8,128)S(1)}, u32[]{:S(2)}, u32[]{:S(2)}) collective-permute-start(f32[8,128]{1,0:T(8,128)} %get-tuple-element.23), channel_id=1, source_target_pairs={{1,0},{2,1},{3,2},{4,3},{5,4},{6,5},{7,6},{8,7},{9,8},{10,9},{11,1... | collective-permute-start | bytes 12296 | tf_op jit(solution)/shard_map/ppermute | solution.py:477
  32.7 0.0 collective-permute-done.6.before
  32.7 0.0 collective-permute-done.7.after
  32.7 0.0 copy-done.1
  32.7 0.0 copy-done.15
  32.8 0.0 copy-done.16
  32.8 0.0 copy-done.17
  32.8 0.0 copy-done.18
  32.8 0.0 copy-done.20
  32.8 0.0 copy-done.24
  32.8 0.0 copy-done.26
  32.8 0.0 copy-start.25
  32.8 1.1 %copy-done.25 = f32[128,3,512]{2,0,1:T(8,128)S(1)} copy-done((f32[128,3,512]{2,0,1:T(8,128)S(1)}, f32[128,3,512]{2,0,1:T(8,128)}, u32[]{:S(2)}) %copy-start.25) | copy-done | bytes 786456
  34.0 0.0 copy-start.9
  34.0 0.0 copy-start.11
  34.0 0.0 copy-start.13
  34.0 4.7 %inner.1 = (f32[5,128,512]{2,1,0:T(8,128)S(1)}, f32[128,512]{1,0:T(8,128)S(1)}, f32[4,128,128]{2,1,0:T(8,128)S(1)}) custom-call(f32[5,128,512]{2,1,0:T(8,128)S(1)} %bitcast.11, f32[3,128,512]{2,1,0:T(8,128)S(1)} %bitcast.18, f32[3,128,512]{2,1,0:T(8,128)S(1)} %bitcast.19, s32[1,128]{1,0:T(1,128)S(1)} %bitcast.14, ...), custom_call_target="tpu_custom_call" | custom-call | flops 4000000000 | bytes 6000000 | tf_op jit(solution)/shard_map/inner/pallas_call | solution.py:363
  38.7 0.0 collective-permute-done.4.before
  38.7 0.0 collective-permute-done.5.after
  38.8 0.0 copy-done.3
  38.8 0.0 copy-done.4
  38.8 0.0 copy-done.5
  38.8 0.0 copy-done.7
  38.8 0.0 copy-done.9
  38.8 0.0 copy-done.11
  38.8 0.0 copy-done.13
  38.8 2.3 %outer.1 = f32[5,128,512]{2,1,0:T(8,128)} custom-call(bf16[320,128]{1,0:T(8,128)(2,1)S(1)} %copy-done.7, bf16[320,128]{1,0:T(8,128)(2,1)S(1)} %copy-done.9, f32[320,128]{1,0:T(8,128)S(1)} %copy-done.3, bf16[320,128]{1,0:T(8,128)(2,1)S(1)} %copy-done.11, bf16[320,128]{1,0:T(8,128)(2,1)S(1)} %copy-done.13, f32[8,128]{1,0:T(8,128)S(1)} %collective-permute-done.4.before, ...), custom_call_target="tpu_custom_call" | custom-call | tf_op jit(solution)/shard_map/outer/pallas_call | solution.py:457
  (11 shorter events, 0.0 us)
Async XLA Ops:
  0.0 1.3 %copy-start = (f32[128,5,512]{2,0,1:T(8,128)S(1)}, f32[128,5,512]{2,0,1:T(8,128)}, u32[]{:S(2)}) copy-start(f32[128,5,512]{2,0,1:T(8,128)} %param.19) | copy-start | bytes 3932164
  1.3 0.9 %copy-start.14 = (bf16[256,512]{1,0:T(8,128)(2,1)S(1)}, bf16[256,512]{1,0:T(8,128)(2,1)}, u32[]{:S(2)}) copy-start(bf16[256,512]{1,0:T(8,128)(2,1)} %constant.16.clone.refs_5_) | copy-start | bytes 786436
  2.3 0.7 %copy-start.19 = (s32[128,1]{0,1:T(1,128)S(1)}, s32[128,1]{0,1:T(1,128)}, u32[]{:S(2)}) copy-start(s32[128,1]{0,1:T(1,128)} %param.25) | copy-start | bytes 1540
  2.9 0.7 %copy-start.21 = (s32[128,1]{0,1:T(1,128)S(1)}, s32[128,1]{0,1:T(1,128)}, u32[]{:S(2)}) copy-start(s32[128,1]{0,1:T(1,128)} %param.22) | copy-start | bytes 1540
  3.6 0.7 %copy-start.22 = (s32[128,1]{0,1:T(1,128)S(1)}, s32[128,1]{0,1:T(1,128)}, u32[]{:S(2)}) copy-start(s32[128,1]{0,1:T(1,128)} %param.23) | copy-start | bytes 1540
  4.2 0.7 %copy-start.23 = (s32[128,1]{0,1:T(1,128)S(1)}, s32[128,1]{0,1:T(1,128)}, u32[]{:S(2)}) copy-start(s32[128,1]{0,1:T(1,128)} %param.24) | copy-start | bytes 1540
  7.4 0.7 %copy-start.2 = (f32[320,128]{1,0:T(8,128)}, f32[320,128]{1,0:T(8,128)S(1)}, u32[]{:S(2)}) copy-start(f32[320,128]{1,0:T(8,128)S(1)} %get-tuple-element.19.own) | copy-start | bytes 491524
  8.1 9.3 %collective-permute-start = (bf16[320,128]{1,0:T(8,128)(2,1)S(1)}, bf16[320,128]{1,0:T(8,128)(2,1)S(1)}, u32[]{:S(2)}, u32[]{:S(2)}) collective-permute-start(bf16[320,128]{1,0:T(8,128)(2,1)S(1)} %get-tuple-element.17), channel_id=1, source_target_pairs={{0,24},{4,28},{8,0},{12,4},{16,8},{20,12},{24,16},{28,20},{1,25},{... | collective-permute-start | bytes 245768 | tf_op jit(solution)/shard_map/ppermute | solution.py:495
  8.5 14.3 %collective-permute-start.1 = (bf16[320,128]{1,0:T(8,128)(2,1)S(1)}, bf16[320,128]{1,0:T(8,128)(2,1)S(1)}, u32[]{:S(2)}, u32[]{:S(2)}) collective-permute-start(bf16[320,128]{1,0:T(8,128)(2,1)S(1)} %get-tuple-element.18), channel_id=1, source_target_pairs={{0,28},{4,0},{8,4},{12,8},{16,12},{20,16},{24,20},{28,24},{1,29},{... | collective-permute-start | bytes 245768 | tf_op jit(solution)/shard_map/ppermute | solution.py:495
  9.9 13.0 %collective-permute-start.2 = (bf16[320,128]{1,0:T(8,128)(2,1)S(1)}, bf16[320,128]{1,0:T(8,128)(2,1)S(1)}, u32[]{:S(2)}, u32[]{:S(2)}) collective-permute-start(bf16[320,128]{1,0:T(8,128)(2,1)S(1)} %get-tuple-element.20), channel_id=1, source_target_pairs={{0,4},{4,8},{8,12},{12,16},{16,20},{20,24},{24,28},{28,0},{1,5},{5... | collective-permute-start | bytes 245768 | tf_op jit(solution)/shard_map/ppermute | solution.py:495
  10.5 22.2 %copy-start.1 = (f32[128,5,512]{2,0,1:T(8,128)S(1)}, f32[128,5,512]{2,0,1:T(8,128)}, u32[]{:S(2)}) copy-start(f32[128,5,512]{2,0,1:T(8,128)} %param.19) | copy-start | bytes 3932164
  10.5 22.2 %copy-start.15 = (bf16[256,256]{1,0:T(8,128)(2,1)S(1)}, bf16[256,256]{1,0:T(8,128)(2,1)}, u32[]{:S(2)}) copy-start(bf16[256,256]{1,0:T(8,128)(2,1)} %constant.19.clone.wb1) | copy-start | bytes 393220
  10.5 22.2 %copy-start.16 = (bf16[256,256]{1,0:T(8,128)(2,1)S(1)}, bf16[256,256]{1,0:T(8,128)(2,1)}, u32[]{:S(2)}) copy-start(bf16[256,256]{1,0:T(8,128)(2,1)} %constant.17.clone.wf1) | copy-start | bytes 393220
  10.5 22.2 %copy-start.17 = (bf16[256,128]{1,0:T(8,128)(2,1)S(1)}, bf16[256,128]{1,0:T(8,128)(2,1)}, u32[]{:S(2)}) copy-start(bf16[256,128]{1,0:T(8,128)(2,1)} %constant.20.clone.wb2) | copy-start | bytes 196612
  10.5 22.2 %copy-start.18 = (bf16[128,256]{1,0:T(8,128)(2,1)S(1)}, bf16[128,256]{1,0:T(8,128)(2,1)}, u32[]{:S(2)}) copy-start(bf16[128,256]{1,0:T(8,128)(2,1)} %constant.18.clone.wf2) | copy-start | bytes 196612
  10.6 22.2 %copy-start.20 = (s32[128,1]{0,1:T(1,128)S(1)}, s32[128,1]{0,1:T(1,128)}, u32[]{:S(2)}) copy-start(s32[128,1]{0,1:T(1,128)} %param.25) | copy-start | bytes 1540
  10.6 22.2 %copy-start.24 = (f32[128,3,512]{2,0,1:T(8,128)S(1)}, f32[128,3,512]{2,0,1:T(8,128)}, u32[]{:S(2)}) copy-start(f32[128,3,512]{2,0,1:T(8,128)} %param.20) | copy-start | bytes 2359300
  10.6 22.2 %copy-start.26 = (f32[40,128]{1,0:T(8,128)S(1)}, f32[40,128]{1,0:T(8,128)}, u32[]{:S(2)}) copy-start(f32[40,128]{1,0:T(8,128)} %constant.21.clone.coef) | copy-start | bytes 61444
  10.6 12.3 %collective-permute-start.3 = (bf16[320,128]{1,0:T(8,128)(2,1)S(1)}, bf16[320,128]{1,0:T(8,128)(2,1)S(1)}, u32[]{:S(2)}, u32[]{:S(2)}) collective-permute-start(bf16[320,128]{1,0:T(8,128)(2,1)S(1)} %get-tuple-element.21), channel_id=1, source_target_pairs={{0,8},{4,12},{8,16},{12,20},{16,24},{20,28},{24,0},{28,4},{1,9},{5... | collective-permute-start | bytes 245768 | tf_op jit(solution)/shard_map/ppermute | solution.py:495
  15.5 17.3 %collective-permute-start.6 = (f32[8,128]{1,0:T(8,128)}, f32[8,128]{1,0:T(8,128)S(1)}, u32[]{:S(2)}, u32[]{:S(2)}) collective-permute-start(f32[8,128]{1,0:T(8,128)} %get-tuple-element.24), channel_id=1, source_target_pairs={{0,1},{1,2},{2,3},{3,4},{4,5},{5,6},{6,7},{7,8},{8,9},{9,10},{10,1... | collective-permute-start | bytes 12296 | tf_op jit(solution)/shard_map/ppermute | solution.py:477
  17.4 5.5 %copy-start.6 = (bf16[320,128]{1,0:T(8,128)(2,1)}, bf16[320,128]{1,0:T(8,128)(2,1)S(1)}, u32[]{:S(2)}) copy-start(bf16[320,128]{1,0:T(8,128)(2,1)S(1)} %collective-permute-done.a) | copy-start | bytes 245764
  17.4 15.3 %collective-permute-start.7 = (f32[8,128]{1,0:T(8,128)}, f32[8,128]{1,0:T(8,128)S(1)}, u32[]{:S(2)}, u32[]{:S(2)}) collective-permute-start(f32[8,128]{1,0:T(8,128)} %get-tuple-element.25), channel_id=1, source_target_pairs={{1,0},{2,1},{3,2},{4,3},{5,4},{6,5},{7,6},{8,7},{9,8},{10,9},{11,1... | collective-permute-start | bytes 12296 | tf_op jit(solution)/shard_map/ppermute | solution.py:477
  22.8 0.6 %copy-start.8 = (bf16[320,128]{1,0:T(8,128)(2,1)}, bf16[320,128]{1,0:T(8,128)(2,1)S(1)}, u32[]{:S(2)}) copy-start(bf16[320,128]{1,0:T(8,128)(2,1)S(1)} %collective-permute-done.1.b) | copy-start | bytes 245764
  22.9 0.6 %copy-start.10 = (bf16[320,128]{1,0:T(8,128)(2,1)}, bf16[320,128]{1,0:T(8,128)(2,1)S(1)}, u32[]{:S(2)}) copy-start(bf16[320,128]{1,0:T(8,128)(2,1)S(1)} %collective-permute-done.2.c) | copy-start | bytes 245764
  22.9 0.6 %copy-start.12 = (bf16[320,128]{1,0:T(8,128)(2,1)}, bf16[320,128]{1,0:T(8,128)(2,1)S(1)}, u32[]{:S(2)}) copy-start(bf16[320,128]{1,0:T(8,128)(2,1)S(1)} %collective-permute-done.3.d) | copy-start | bytes 245764
  25.4 13.4 %collective-permute-start.4 = (f32[8,128]{1,0:T(8,128)}, f32[8,128]{1,0:T(8,128)S(1)}, u32[]{:S(2)}, u32[]{:S(2)}) collective-permute-start(f32[8,128]{1,0:T(8,128)} %get-tuple-element.22), channel_id=1, source_target_pairs={{0,1},{1,2},{2,3},{3,4},{4,5},{5,6},{6,7},{7,8},{8,9},{9,10},{10,1... | collective-permute-start | bytes 12296 | tf_op jit(solution)/shard_map/ppermute | solution.py:477
  27.3 11.5 %collective-permute-start.5 = (f32[8,128]{1,0:T(8,128)}, f32[8,128]{1,0:T(8,128)S(1)}, u32[]{:S(2)}, u32[]{:S(2)}) collective-permute-start(f32[8,128]{1,0:T(8,128)} %get-tuple-element.23), channel_id=1, source_target_pairs={{1,0},{2,1},{3,2},{4,3},{5,4},{6,5},{7,6},{8,7},{9,8},{10,9},{11,1... | collective-permute-start | bytes 12296 | tf_op jit(solution)/shard_map/ppermute | solution.py:477
  32.8 1.1 %copy-start.25 = (f32[128,3,512]{2,0,1:T(8,128)S(1)}, f32[128,3,512]{2,0,1:T(8,128)}, u32[]{:S(2)}) copy-start(f32[128,3,512]{2,0,1:T(8,128)} %param.21) | copy-start | bytes 2359300
  34.0 4.8 %copy-start.3 = (f32[320,128]{1,0:T(8,128)S(1)}, f32[320,128]{1,0:T(8,128)}, u32[]{:S(2)}) copy-start(f32[320,128]{1,0:T(8,128)} %copy-done.2) | copy-start | bytes 491524
  34.0 4.8 %copy-start.4 = (bf16[256,1024]{1,0:T(8,128)(2,1)S(1)}, bf16[256,1024]{1,0:T(8,128)(2,1)}, u32[]{:S(2)}) copy-start(bf16[256,1024]{1,0:T(8,128)(2,1)} %constant.23.clone.place) | copy-start | bytes 1572868
  34.0 4.8 %copy-start.5 = (bf16[256,1024]{1,0:T(8,128)(2,1)S(1)}, bf16[256,1024]{1,0:T(8,128)(2,1)}, u32[]{:S(2)}) copy-start(bf16[256,1024]{1,0:T(8,128)(2,1)} %constant.22.clone.spread) | copy-start | bytes 1572868
  34.0 4.8 %copy-start.7 = (bf16[320,128]{1,0:T(8,128)(2,1)S(1)}, bf16[320,128]{1,0:T(8,128)(2,1)}, u32[]{:S(2)}) copy-start(bf16[320,128]{1,0:T(8,128)(2,1)} %copy-done.6) | copy-start | bytes 245764
  34.0 4.8 %copy-start.9 = (bf16[320,128]{1,0:T(8,128)(2,1)S(1)}, bf16[320,128]{1,0:T(8,128)(2,1)}, u32[]{:S(2)}) copy-start(bf16[320,128]{1,0:T(8,128)(2,1)} %copy-done.8) | copy-start | bytes 245764
  34.0 4.8 %copy-start.11 = (bf16[320,128]{1,0:T(8,128)(2,1)S(1)}, bf16[320,128]{1,0:T(8,128)(2,1)}, u32[]{:S(2)}) copy-start(bf16[320,128]{1,0:T(8,128)(2,1)} %copy-done.10) | copy-start | bytes 245764
  34.0 4.8 %copy-start.13 = (bf16[320,128]{1,0:T(8,128)(2,1)S(1)}, bf16[320,128]{1,0:T(8,128)(2,1)}, u32[]{:S(2)}) copy-start(bf16[320,128]{1,0:T(8,128)(2,1)} %copy-done.12) | copy-start | bytes 245764
